TPU v7x, 32 devices: a whole 2x2x4 slice. The times are simulated.
32 devices in a mesh: section: 4 (over y, x), dp: 8 (over z, core).
Axes of the slice: x: 2, y: 2, z: 4, core: 2. Of those that a mesh axis runs over, the one named last changes fastest.
Arguments:
- inputs: bfloat16 [61440, 512], P('dp'), may hold values from -6 to 6
- cotangent: bfloat16 [61440, 512], P('dp'), may hold values from -6 to 6
- latent_codes: bfloat16 [64, 256], replicated, may hold values from -6 to 6
- positions: bfloat16 [3, 61440], P(None, 'dp'), may hold values from -1 to 1
- shape_ids: int32 [61440], P('dp'), may hold values from 0 to 63
- direction_first: bfloat16 [4, 771, 512], P('section'), may hold values from -0.21875 to 0.21875
- gain_first: bfloat16 [4, 512], P('section'), may hold values from 0.099609375 to 1.8984375
- bias_first: bfloat16 [4, 512], P('section'), may hold values from -3 to 3
- direction_second: bfloat16 [4, 512, 512], P('section'), may hold values from -0.25 to 0.25
- gain_second: bfloat16 [4, 512], P('section'), may hold values from 0.099609375 to 1.8984375
- bias_second: bfloat16 [4, 512], P('section'), may hold values from -3 to 3
Outputs:
- activations: bfloat16 [4, 61440, 512], P('section', 'dp')
- input_grads: bfloat16 [4, 61440, 512], P('section', 'dp')
- code_grad: float32 [64, 256], P(('section', 'dp'))
- direction_first_grad: float32 [4, 771, 512], P('section')
- gain_first_grad: float32 [4, 512], P('section')
- bias_first_grad: float32 [4, 512], P('section')
- direction_second_grad: float32 [4, 512, 512], P('section')
- gain_second_grad: float32 [4, 512], P('section')
- bias_second_grad: float32 [4, 512], P('section')
All inputs are finite; a program needn't handle non-finite values.
Results may differ from a plain program's by a relative error of at most 0.0095.
Values may be sent and summed in bfloat16 or wider, within the bound.
No kernel may reach another device: no remote copies, remote signals or barrier semaphores. Data moves between devices by JAX's collectives and lax.ppermute only.
A program may use at most 128 MiB of HBM per device.

v0:
```python
import jax
import jax.numpy as jnp
from jax import lax
from jax.sharding import PartitionSpec as P

MICRO = 6


def passed_along(block, axis, distance):
    devices = range(lax.axis_size(axis))
    route = [(i - distance, i) for i in devices if i - distance in devices]
    return lax.ppermute(block, axis, route)


def norm_weight(direction, gain_row):
    column_scale = gain_row / jnp.sqrt(jnp.sum(direction * direction, axis=0) + 1e-06)
    return direction * column_scale[None, :]


def weight_pullback(direction, gain_row, summed):
    unused, pullback = jax.vjp(norm_weight, direction, gain_row)
    return pullback(summed)


def silu_slope(values):
    sigmoid_part = jax.nn.sigmoid(values)
    return sigmoid_part * (1.0 + values * (1.0 - sigmoid_part))


def contract_rows(left_side, right_side):
    return lax.dot_general(
        left_side, right_side, (((0,), (0,)), ((), ())), preferred_element_type=jnp.float32
    )


def contract_cols(left_side, right_side):
    return lax.dot_general(
        left_side, right_side, (((1,), (1,)), ((), ())), preferred_element_type=jnp.float32
    )


def write_rows(target, block, first_row, active_tick):
    former = lax.dynamic_slice_in_dim(target, first_row, block.shape[0], 0)
    chosen = jnp.where(active_tick, block, former)
    return lax.dynamic_update_slice_in_dim(target, chosen, first_row, 0)


def layer_pair(
    entering, skip_rows, place_rows, weight_first, weight_second, offset_first, offset_second
):
    joined = jnp.concatenate([entering, skip_rows, place_rows.T], axis=1)
    inner_sum = (
        jnp.dot(joined, weight_first, preferred_element_type=jnp.float32) + offset_first[None, :]
    )
    active = jax.nn.silu(inner_sum).astype(jnp.bfloat16)
    outer_sum = (
        jnp.dot(active, weight_second, preferred_element_type=jnp.float32) + offset_second[None, :]
    )
    return (joined, inner_sum, active, outer_sum)


def pair_backward(
    arriving, joined, inner_sum, active, outer_sum, weight_first, weight_second, width, latent
):
    outer_grad = (arriving.astype(jnp.float32) * silu_slope(outer_sum)).astype(jnp.bfloat16)
    active_grad = contract_cols(outer_grad, weight_second)
    inner_grad = (active_grad * silu_slope(inner_sum)).astype(jnp.bfloat16)
    joined_grad = contract_cols(inner_grad, weight_first)
    leaving = joined_grad[:, :width].astype(jnp.bfloat16)
    skip_grad = joined_grad[:, width : width + latent].astype(jnp.bfloat16)
    grad_first = contract_rows(joined, inner_grad)
    grad_second = contract_rows(active, outer_grad)
    bias_grad_first = jnp.sum(inner_grad.astype(jnp.float32), axis=0)
    bias_grad_second = jnp.sum(outer_grad.astype(jnp.float32), axis=0)
    return (leaving, skip_grad, grad_first, grad_second, bias_grad_first, bias_grad_second)


def shards(
    inputs,
    cotangent,
    latent_codes,
    positions,
    shape_ids,
    direction_first,
    gain_first,
    bias_first,
    direction_second,
    gain_second,
    bias_second,
):
    section_count = lax.axis_size("section")
    section_rank = lax.axis_index("section")
    total_rows, width = inputs.shape
    shape_count, latent = latent_codes.shape
    dir_first = direction_first[0].astype(jnp.float32)
    dir_second = direction_second[0].astype(jnp.float32)
    gains_first = gain_first[0].astype(jnp.float32)
    gains_second = gain_second[0].astype(jnp.float32)
    shape_range = jnp.arange(shape_count, dtype=jnp.int32)

    def skip_block(first_row, row_count):
        point_shapes = lax.dynamic_slice_in_dim(shape_ids, first_row, row_count, 0)
        onehot = (point_shapes[:, None] == shape_range[None, :]).astype(jnp.bfloat16)
        place_rows = lax.dynamic_slice_in_dim(positions, first_row, row_count, 1)
        skip_rows = jnp.dot(onehot, latent_codes, preferred_element_type=jnp.float32).astype(
            jnp.bfloat16
        )
        return (onehot, place_rows, skip_rows)

    piece_rows = total_rows // MICRO
    ticks = MICRO + section_count - 1
    offset_first = bias_first[0].astype(jnp.float32)
    offset_second = bias_second[0].astype(jnp.float32)
    weight_first = norm_weight(dir_first, gains_first).astype(jnp.bfloat16)
    weight_second = norm_weight(dir_second, gains_second).astype(jnp.bfloat16)

    def forward_tick(tick_index, carry):
        incoming, stored, outputs = carry
        micro_index = tick_index - section_rank
        active_tick = (micro_index >= 0) & (micro_index < MICRO)
        first_row = jnp.clip(micro_index, 0, MICRO - 1) * piece_rows
        fresh = lax.dynamic_slice_in_dim(inputs, first_row, piece_rows, 0)
        entering = jnp.where(section_rank == 0, fresh, incoming)
        onehot, place_rows, skip_rows = skip_block(first_row, piece_rows)
        joined, inner_sum, active, outer_sum = layer_pair(
            entering,
            skip_rows,
            place_rows,
            weight_first,
            weight_second,
            offset_first,
            offset_second,
        )
        leaving = jax.nn.silu(outer_sum).astype(jnp.bfloat16)
        stored = write_rows(stored, entering, first_row, active_tick)
        outputs = write_rows(outputs, leaving, first_row, active_tick)
        incoming = passed_along(leaving, "section", 1)
        return (incoming, stored, outputs)

    empty_rows = jnp.zeros((piece_rows, width), jnp.bfloat16)
    empty_all = jnp.zeros((total_rows, width), jnp.bfloat16)
    unused, stored, outputs = lax.fori_loop(
        0, ticks, forward_tick, (empty_rows, empty_all, empty_all)
    )

    def backward_tick(tick_index, carry):
        (
            incoming,
            grad_rows,
            grad_first,
            grad_second,
            bias_grad_first,
            bias_grad_second,
            code_partial,
        ) = carry
        micro_index = tick_index - (section_count - 1 - section_rank)
        active_tick = (micro_index >= 0) & (micro_index < MICRO)
        first_row = jnp.clip(micro_index, 0, MICRO - 1) * piece_rows
        entering = lax.dynamic_slice_in_dim(stored, first_row, piece_rows, 0)
        given = lax.dynamic_slice_in_dim(cotangent, first_row, piece_rows, 0)
        arriving = jnp.where(section_rank == section_count - 1, given, incoming)
        arriving = jnp.where(active_tick, arriving, jnp.zeros_like(arriving))
        onehot, place_rows, skip_rows = skip_block(first_row, piece_rows)
        joined, inner_sum, active, outer_sum = layer_pair(
            entering,
            skip_rows,
            place_rows,
            weight_first,
            weight_second,
            offset_first,
            offset_second,
        )
        leaving, skip_grad, part_first, part_second, part_bias_first, part_bias_second = (
            pair_backward(
                arriving,
                joined,
                inner_sum,
                active,
                outer_sum,
                weight_first,
                weight_second,
                width,
                latent,
            )
        )
        grad_first = grad_first + part_first
        grad_second = grad_second + part_second
        bias_grad_first = bias_grad_first + part_bias_first
        bias_grad_second = bias_grad_second + part_bias_second
        code_partial = code_partial + contract_rows(onehot, skip_grad)
        grad_rows = write_rows(grad_rows, leaving, first_row, active_tick)
        incoming = passed_along(leaving, "section", -1)
        return (
            incoming,
            grad_rows,
            grad_first,
            grad_second,
            bias_grad_first,
            bias_grad_second,
            code_partial,
        )

    start_carry = (
        empty_rows,
        empty_all,
        jnp.zeros(dir_first.shape, jnp.float32),
        jnp.zeros(dir_second.shape, jnp.float32),
        jnp.zeros((width,), jnp.float32),
        jnp.zeros((width,), jnp.float32),
        jnp.zeros((shape_count, latent), jnp.float32),
    )
    ending = lax.fori_loop(0, ticks, backward_tick, start_carry)
    unused, grad_rows, grad_first, grad_second, bias_grad_first, bias_grad_second, code_partial = (
        ending
    )
    sum_first, sum_second, bias_sum_first, bias_sum_second = lax.psum(
        (grad_first, grad_second, bias_grad_first, bias_grad_second), "dp"
    )
    dir_grad_first, gain_grad_first = weight_pullback(dir_first, gains_first, sum_first)
    dir_grad_second, gain_grad_second = weight_pullback(dir_second, gains_second, sum_second)
    code_total = lax.psum_scatter(code_partial, ("section", "dp"), scatter_dimension=0, tiled=True)
    return (
        outputs[None],
        grad_rows[None],
        code_total,
        dir_grad_first[None],
        gain_grad_first[None],
        bias_sum_first[None],
        dir_grad_second[None],
        gain_grad_second[None],
        bias_sum_second[None],
    )


def solution(mesh):
    in_specs = (
        P("dp", None),
        P("dp", None),
        P(),
        P(None, "dp"),
        P("dp"),
        P("section", None, None),
        P("section", None),
        P("section", None),
        P("section", None, None),
        P("section", None),
        P("section", None),
    )
    out_specs = (
        P("section", "dp", None),
        P("section", "dp", None),
        P(("section", "dp"), None),
        P("section", None, None),
        P("section", None),
        P("section", None),
        P("section", None, None),
        P("section", None),
        P("section", None),
    )
    return jax.shard_map(shards, mesh=mesh, in_specs=in_specs, out_specs=out_specs, check_vma=False)
```

profile of v0, /device:TPU:0, one launch (start us, length us, event | category | flops | bytes accessed | tf_op | source)
XLA Modules:
  0.0 994.0 jit_solution(8196542614412268453)
XLA Ops:
  24.3 372.5 %while.47 = (s32[]{:T(128)}, bf16[1280,512]{1,0:T(8,128)(2,1)S(1)}, bf16[7680,512]{1,0:T(8,128)(2,1)}, bf16[7680,512]{1,0:T(8,128)(2,1)}, pred[]{:T(512)}, /*ind...) while((s32[]{:T(128)}, bf16[1280,512]{1,0:T(8,128)(2,1)S(1)}, ...), condition=%wide.region_3.4_spmd.clone, body=%wide.region_2.3_spmd.clone.sunk | while | flops 1739758080 | bytes 20065108 | solution.py:142
  41.0 28.2 %collective-permute-done = bf16[1280,512]{1,0:T(8,128)(2,1)S(1)} collective-permute-done((bf16[1280,512]{1,0:T(8,128)(2,1)}, bf16[1280,512]{1,0:T(8,128)(2,1)S(1)}, u32[]{:S(2)}, u32[]{:S(2)}) %collective-permute-start) | collective-permute-done | bytes 1310752 | tf_op jit(solution)/shard_map/while/body/eval_jaxpr/ppermute | solution.py:12
  85.3 27.4 %collective-permute-done = bf16[1280,512]{1,0:T(8,128)(2,1)S(1)} collective-permute-done((bf16[1280,512]{1,0:T(8,128)(2,1)}, bf16[1280,512]{1,0:T(8,128)(2,1)S(1)}, u32[]{:S(2)}, u32[]{:S(2)}) %collective-permute-start) | collective-permute-done | bytes 1310752 | tf_op jit(solution)/shard_map/while/body/eval_jaxpr/ppermute | solution.py:12
  128.8 26.5 %collective-permute-done = bf16[1280,512]{1,0:T(8,128)(2,1)S(1)} collective-permute-done((bf16[1280,512]{1,0:T(8,128)(2,1)}, bf16[1280,512]{1,0:T(8,128)(2,1)S(1)}, u32[]{:S(2)}, u32[]{:S(2)}) %collective-permute-start) | collective-permute-done | bytes 1310752 | tf_op jit(solution)/shard_map/while/body/eval_jaxpr/ppermute | solution.py:12
  172.3 25.5 %collective-permute-done = bf16[1280,512]{1,0:T(8,128)(2,1)S(1)} collective-permute-done((bf16[1280,512]{1,0:T(8,128)(2,1)}, bf16[1280,512]{1,0:T(8,128)(2,1)S(1)}, u32[]{:S(2)}, u32[]{:S(2)}) %collective-permute-start) | collective-permute-done | bytes 1310752 | tf_op jit(solution)/shard_map/while/body/eval_jaxpr/ppermute | solution.py:12
  203.4 6.2 select_dynamic-update-slice_fusion.7
  214.9 24.6 %collective-permute-done = bf16[1280,512]{1,0:T(8,128)(2,1)S(1)} collective-permute-done((bf16[1280,512]{1,0:T(8,128)(2,1)}, bf16[1280,512]{1,0:T(8,128)(2,1)S(1)}, u32[]{:S(2)}, u32[]{:S(2)}) %collective-permute-start) | collective-permute-done | bytes 1310752 | tf_op jit(solution)/shard_map/while/body/eval_jaxpr/ppermute | solution.py:12
  256.5 23.7 %collective-permute-done = bf16[1280,512]{1,0:T(8,128)(2,1)S(1)} collective-permute-done((bf16[1280,512]{1,0:T(8,128)(2,1)}, bf16[1280,512]{1,0:T(8,128)(2,1)S(1)}, u32[]{:S(2)}, u32[]{:S(2)}) %collective-permute-start) | collective-permute-done | bytes 1310752 | tf_op jit(solution)/shard_map/while/body/eval_jaxpr/ppermute | solution.py:12
  297.2 22.7 %collective-permute-done = bf16[1280,512]{1,0:T(8,128)(2,1)S(1)} collective-permute-done((bf16[1280,512]{1,0:T(8,128)(2,1)}, bf16[1280,512]{1,0:T(8,128)(2,1)S(1)}, u32[]{:S(2)}, u32[]{:S(2)}) %collective-permute-start) | collective-permute-done | bytes 1310752 | tf_op jit(solution)/shard_map/while/body/eval_jaxpr/ppermute | solution.py:12
  337.0 21.8 %collective-permute-done = bf16[1280,512]{1,0:T(8,128)(2,1)S(1)} collective-permute-done((bf16[1280,512]{1,0:T(8,128)(2,1)}, bf16[1280,512]{1,0:T(8,128)(2,1)S(1)}, u32[]{:S(2)}, u32[]{:S(2)}) %collective-permute-start) | collective-permute-done | bytes 1310752 | tf_op jit(solution)/shard_map/while/body/eval_jaxpr/ppermute | solution.py:12
  375.9 20.9 %collective-permute-done = bf16[1280,512]{1,0:T(8,128)(2,1)S(1)} collective-permute-done((bf16[1280,512]{1,0:T(8,128)(2,1)}, bf16[1280,512]{1,0:T(8,128)(2,1)S(1)}, u32[]{:S(2)}, u32[]{:S(2)}) %collective-permute-start) | collective-permute-done | bytes 1310752 | tf_op jit(solution)/shard_map/while/body/eval_jaxpr/ppermute | solution.py:12
  401.7 384.5 %while.48 = (s32[]{:T(128)}, bf16[1280,512]{1,0:T(8,128)(2,1)}, bf16[7680,512]{1,0:T(8,128)(2,1)}, f32[771,512]{1,0:T(8,128)}, f32[512,512]{1,0:T(8,128)}, /*ind...) while((s32[]{:T(128)}, bf16[1280,512]{1,0:T(8,128)(2,1)}, ...), condition=%wide.region_7.8_spmd.clone, body=%wide.region_4.7_spmd.clone.sunk | while | flops 5168419840 | bytes 103739528 | solution.py:212
  430.1 17.8 %collective-permute-done.1 = bf16[1280,512]{1,0:T(8,128)(2,1)} collective-permute-done((bf16[1280,512]{1,0:T(8,128)(2,1)S(1)}, bf16[1280,512]{1,0:T(8,128)(2,1)}, u32[]{:S(2)}, u32[]{:S(2)}) %collective-permute-start.1) | collective-permute-done | bytes 1310752 | tf_op jit(solution)/shard_map/while/body/eval_jaxpr/ppermute | solution.py:12
  476.8 16.6 %collective-permute-done.1 = bf16[1280,512]{1,0:T(8,128)(2,1)} collective-permute-done((bf16[1280,512]{1,0:T(8,128)(2,1)S(1)}, bf16[1280,512]{1,0:T(8,128)(2,1)}, u32[]{:S(2)}, u32[]{:S(2)}) %collective-permute-start.1) | collective-permute-done | bytes 1310752 | tf_op jit(solution)/shard_map/while/body/eval_jaxpr/ppermute | solution.py:12
  522.3 15.1 %collective-permute-done.1 = bf16[1280,512]{1,0:T(8,128)(2,1)} collective-permute-done((bf16[1280,512]{1,0:T(8,128)(2,1)S(1)}, bf16[1280,512]{1,0:T(8,128)(2,1)}, u32[]{:S(2)}, u32[]{:S(2)}) %collective-permute-start.1) | collective-permute-done | bytes 1310752 | tf_op jit(solution)/shard_map/while/body/eval_jaxpr/ppermute | solution.py:12
  566.3 14.1 %collective-permute-done.1 = bf16[1280,512]{1,0:T(8,128)(2,1)} collective-permute-done((bf16[1280,512]{1,0:T(8,128)(2,1)S(1)}, bf16[1280,512]{1,0:T(8,128)(2,1)}, u32[]{:S(2)}, u32[]{:S(2)}) %collective-permute-start.1) | collective-permute-done | bytes 1310752 | tf_op jit(solution)/shard_map/while/body/eval_jaxpr/ppermute | solution.py:12
  609.3 13.2 %collective-permute-done.1 = bf16[1280,512]{1,0:T(8,128)(2,1)} collective-permute-done((bf16[1280,512]{1,0:T(8,128)(2,1)S(1)}, bf16[1280,512]{1,0:T(8,128)(2,1)}, u32[]{:S(2)}, u32[]{:S(2)}) %collective-permute-start.1) | collective-permute-done | bytes 1310752 | tf_op jit(solution)/shard_map/while/body/eval_jaxpr/ppermute | solution.py:12
  651.5 12.3 %collective-permute-done.1 = bf16[1280,512]{1,0:T(8,128)(2,1)} collective-permute-done((bf16[1280,512]{1,0:T(8,128)(2,1)S(1)}, bf16[1280,512]{1,0:T(8,128)(2,1)}, u32[]{:S(2)}, u32[]{:S(2)}) %collective-permute-start.1) | collective-permute-done | bytes 1310752 | tf_op jit(solution)/shard_map/while/body/eval_jaxpr/ppermute | solution.py:12
  692.7 11.7 %collective-permute-done.1 = bf16[1280,512]{1,0:T(8,128)(2,1)} collective-permute-done((bf16[1280,512]{1,0:T(8,128)(2,1)S(1)}, bf16[1280,512]{1,0:T(8,128)(2,1)}, u32[]{:S(2)}, u32[]{:S(2)}) %collective-permute-start.1) | collective-permute-done | bytes 1310752 | tf_op jit(solution)/shard_map/while/body/eval_jaxpr/ppermute | solution.py:12
  733.3 12.0 %collective-permute-done.1 = bf16[1280,512]{1,0:T(8,128)(2,1)} collective-permute-done((bf16[1280,512]{1,0:T(8,128)(2,1)S(1)}, bf16[1280,512]{1,0:T(8,128)(2,1)}, u32[]{:S(2)}, u32[]{:S(2)}) %collective-permute-start.1) | collective-permute-done | bytes 1310752 | tf_op jit(solution)/shard_map/while/body/eval_jaxpr/ppermute | solution.py:12
  774.2 12.0 %collective-permute-done.1 = bf16[1280,512]{1,0:T(8,128)(2,1)} collective-permute-done((bf16[1280,512]{1,0:T(8,128)(2,1)S(1)}, bf16[1280,512]{1,0:T(8,128)(2,1)}, u32[]{:S(2)}, u32[]{:S(2)}) %collective-permute-start.1) | collective-permute-done | bytes 1310752 | tf_op jit(solution)/shard_map/while/body/eval_jaxpr/ppermute | solution.py:12
  787.6 14.2 %all-reduce.1 = (f32[1,512]{1,0:T(1,128)}, f32[1,512]{1,0:T(1,128)}) all-reduce(f32[1,512]{1,0:T(1,128)S(1)} %bitcast.75, f32[1,512]{1,0:T(1,128)S(1)} %bitcast.74), channel_id=1, replica_groups=mesh['section'=4,'dp'=8] {'dp'}, use_global_device_ids=true, to_apply=%region_11.12 | all-reduce | flops 1024 | bytes 8192 | tf_op jit(solution)/shard_map/psum | solution.py:216
  801.9 104.8 %all-reduce.6.cloned.1.call-done = f32[64,256]{1,0:T(8,128)} async-done(((f32[64,256]{1,0:T(8,128)}), f32[64,256]{1,0:T(8,128)}) %all-reduce.6.cloned.1.call-update) | async-done | bytes 65552
  907.9 72.1 %all-reduce.8.cloned.1.call-done = (f32[771,512]{1,0:T(8,128)}, f32[512,512]{1,0:T(8,128)}) async-done(((f32[771,512]{1,0:T(8,128)}, f32[512,512]{1,0:T(8,128)}), (f32[771,512]{1,0:T(8,128)}, f32[512,512]{1,0:T(8,128)})) %all-reduce.8.cloned.1.call-update) | async-done | bytes 2627600 | tf_op jit(solution)/shard_map/psum | solution.py:216
  (435 shorter events, 434.1 us)
Async XLA Ops:
  7.2 899.4 %all-reduce.6.cloned.1.call-start = ((), (), s32[]{:S(2)}) async-start(), calls=%async_computation | async-start | bytes 131072
  36.0 33.2 %collective-permute-start = (bf16[1280,512]{1,0:T(8,128)(2,1)}, bf16[1280,512]{1,0:T(8,128)(2,1)S(1)}, u32[]{:S(2)}, u32[]{:S(2)}) collective-permute-start(bf16[1280,512]{1,0:T(8,128)(2,1)} %get-tuple-element.1174), channel_id=1, source_target_pairs={{0,8},{8,16},{16,24},{1,9},{9,17},{17,25},{2,10},{10,18},{18,26},{... | collective-permute-start | bytes 3932168 | tf_op jit(solution)/shard_map/while/body/eval_jaxpr/ppermute | solution.py:12
  81.0 31.7 %collective-permute-start = (bf16[1280,512]{1,0:T(8,128)(2,1)}, bf16[1280,512]{1,0:T(8,128)(2,1)S(1)}, u32[]{:S(2)}, u32[]{:S(2)}) collective-permute-start(bf16[1280,512]{1,0:T(8,128)(2,1)} %get-tuple-element.1174), channel_id=1, source_target_pairs={{0,8},{8,16},{16,24},{1,9},{9,17},{17,25},{2,10},{10,18},{18,26},{... | collective-permute-start | bytes 3932168 | tf_op jit(solution)/shard_map/while/body/eval_jaxpr/ppermute | solution.py:12
  124.5 30.8 %collective-permute-start = (bf16[1280,512]{1,0:T(8,128)(2,1)}, bf16[1280,512]{1,0:T(8,128)(2,1)S(1)}, u32[]{:S(2)}, u32[]{:S(2)}) collective-permute-start(bf16[1280,512]{1,0:T(8,128)(2,1)} %get-tuple-element.1174), channel_id=1, source_target_pairs={{0,8},{8,16},{16,24},{1,9},{9,17},{17,25},{2,10},{10,18},{18,26},{... | collective-permute-start | bytes 3932168 | tf_op jit(solution)/shard_map/while/body/eval_jaxpr/ppermute | solution.py:12
  167.1 30.8 %collective-permute-start = (bf16[1280,512]{1,0:T(8,128)(2,1)}, bf16[1280,512]{1,0:T(8,128)(2,1)S(1)}, u32[]{:S(2)}, u32[]{:S(2)}) collective-permute-start(bf16[1280,512]{1,0:T(8,128)(2,1)} %get-tuple-element.1174), channel_id=1, source_target_pairs={{0,8},{8,16},{16,24},{1,9},{9,17},{17,25},{2,10},{10,18},{18,26},{... | collective-permute-start | bytes 3932168 | tf_op jit(solution)/shard_map/while/body/eval_jaxpr/ppermute | solution.py:12
  209.6 29.8 %collective-permute-start = (bf16[1280,512]{1,0:T(8,128)(2,1)}, bf16[1280,512]{1,0:T(8,128)(2,1)S(1)}, u32[]{:S(2)}, u32[]{:S(2)}) collective-permute-start(bf16[1280,512]{1,0:T(8,128)(2,1)} %get-tuple-element.1174), channel_id=1, source_target_pairs={{0,8},{8,16},{16,24},{1,9},{9,17},{17,25},{2,10},{10,18},{18,26},{... | collective-permute-start | bytes 3932168 | tf_op jit(solution)/shard_map/while/body/eval_jaxpr/ppermute | solution.py:12
  251.2 29.0 %collective-permute-start = (bf16[1280,512]{1,0:T(8,128)(2,1)}, bf16[1280,512]{1,0:T(8,128)(2,1)S(1)}, u32[]{:S(2)}, u32[]{:S(2)}) collective-permute-start(bf16[1280,512]{1,0:T(8,128)(2,1)} %get-tuple-element.1174), channel_id=1, source_target_pairs={{0,8},{8,16},{16,24},{1,9},{9,17},{17,25},{2,10},{10,18},{18,26},{... | collective-permute-start | bytes 3932168 | tf_op jit(solution)/shard_map/while/body/eval_jaxpr/ppermute | solution.py:12
  292.0 28.0 %collective-permute-start = (bf16[1280,512]{1,0:T(8,128)(2,1)}, bf16[1280,512]{1,0:T(8,128)(2,1)S(1)}, u32[]{:S(2)}, u32[]{:S(2)}) collective-permute-start(bf16[1280,512]{1,0:T(8,128)(2,1)} %get-tuple-element.1174), channel_id=1, source_target_pairs={{0,8},{8,16},{16,24},{1,9},{9,17},{17,25},{2,10},{10,18},{18,26},{... | collective-permute-start | bytes 3932168 | tf_op jit(solution)/shard_map/while/body/eval_jaxpr/ppermute | solution.py:12
  331.7 27.1 %collective-permute-start = (bf16[1280,512]{1,0:T(8,128)(2,1)}, bf16[1280,512]{1,0:T(8,128)(2,1)S(1)}, u32[]{:S(2)}, u32[]{:S(2)}) collective-permute-start(bf16[1280,512]{1,0:T(8,128)(2,1)} %get-tuple-element.1174), channel_id=1, source_target_pairs={{0,8},{8,16},{16,24},{1,9},{9,17},{17,25},{2,10},{10,18},{18,26},{... | collective-permute-start | bytes 3932168 | tf_op jit(solution)/shard_map/while/body/eval_jaxpr/ppermute | solution.py:12
  370.6 26.2 %collective-permute-start = (bf16[1280,512]{1,0:T(8,128)(2,1)}, bf16[1280,512]{1,0:T(8,128)(2,1)S(1)}, u32[]{:S(2)}, u32[]{:S(2)}) collective-permute-start(bf16[1280,512]{1,0:T(8,128)(2,1)} %get-tuple-element.1174), channel_id=1, source_target_pairs={{0,8},{8,16},{16,24},{1,9},{9,17},{17,25},{2,10},{10,18},{18,26},{... | collective-permute-start | bytes 3932168 | tf_op jit(solution)/shard_map/while/body/eval_jaxpr/ppermute | solution.py:12
  422.1 25.8 %collective-permute-start.1 = (bf16[1280,512]{1,0:T(8,128)(2,1)S(1)}, bf16[1280,512]{1,0:T(8,128)(2,1)}, u32[]{:S(2)}, u32[]{:S(2)}) collective-permute-start(bf16[1280,512]{1,0:T(8,128)(2,1)S(1)} %get-tuple-element.1198), channel_id=1, source_target_pairs={{8,0},{16,8},{24,16},{9,1},{17,9},{25,17},{10,2},{18,10},{26,18},{... | collective-permute-start | bytes 3932168 | tf_op jit(solution)/shard_map/while/body/eval_jaxpr/ppermute | solution.py:12
  430.1 17.8 %copy-start.9 = (f32[512,512]{1,0:T(8,128)}, f32[512,512]{1,0:T(8,128)S(1)}, u32[]{:S(2)}) copy-start(f32[512,512]{1,0:T(8,128)S(1)} %convolution_add_fusion.10) | copy-start | bytes 3145732 | tf_op jit(solution)/shard_map/while
  468.3 25.1 %collective-permute-start.1 = (bf16[1280,512]{1,0:T(8,128)(2,1)S(1)}, bf16[1280,512]{1,0:T(8,128)(2,1)}, u32[]{:S(2)}, u32[]{:S(2)}) collective-permute-start(bf16[1280,512]{1,0:T(8,128)(2,1)S(1)} %get-tuple-element.1198), channel_id=1, source_target_pairs={{8,0},{16,8},{24,16},{9,1},{17,9},{25,17},{10,2},{18,10},{26,18},{... | collective-permute-start | bytes 3932168 | tf_op jit(solution)/shard_map/while/body/eval_jaxpr/ppermute | solution.py:12
  513.8 23.6 %collective-permute-start.1 = (bf16[1280,512]{1,0:T(8,128)(2,1)S(1)}, bf16[1280,512]{1,0:T(8,128)(2,1)}, u32[]{:S(2)}, u32[]{:S(2)}) collective-permute-start(bf16[1280,512]{1,0:T(8,128)(2,1)S(1)} %get-tuple-element.1198), channel_id=1, source_target_pairs={{8,0},{16,8},{24,16},{9,1},{17,9},{25,17},{10,2},{18,10},{26,18},{... | collective-permute-start | bytes 3932168 | tf_op jit(solution)/shard_map/while/body/eval_jaxpr/ppermute | solution.py:12
  557.8 22.6 %collective-permute-start.1 = (bf16[1280,512]{1,0:T(8,128)(2,1)S(1)}, bf16[1280,512]{1,0:T(8,128)(2,1)}, u32[]{:S(2)}, u32[]{:S(2)}) collective-permute-start(bf16[1280,512]{1,0:T(8,128)(2,1)S(1)} %get-tuple-element.1198), channel_id=1, source_target_pairs={{8,0},{16,8},{24,16},{9,1},{17,9},{25,17},{10,2},{18,10},{26,18},{... | collective-permute-start | bytes 3932168 | tf_op jit(solution)/shard_map/while/body/eval_jaxpr/ppermute | solution.py:12
  600.8 21.7 %collective-permute-start.1 = (bf16[1280,512]{1,0:T(8,128)(2,1)S(1)}, bf16[1280,512]{1,0:T(8,128)(2,1)}, u32[]{:S(2)}, u32[]{:S(2)}) collective-permute-start(bf16[1280,512]{1,0:T(8,128)(2,1)S(1)} %get-tuple-element.1198), channel_id=1, source_target_pairs={{8,0},{16,8},{24,16},{9,1},{17,9},{25,17},{10,2},{18,10},{26,18},{... | collective-permute-start | bytes 3932168 | tf_op jit(solution)/shard_map/while/body/eval_jaxpr/ppermute | solution.py:12
  643.0 20.8 %collective-permute-start.1 = (bf16[1280,512]{1,0:T(8,128)(2,1)S(1)}, bf16[1280,512]{1,0:T(8,128)(2,1)}, u32[]{:S(2)}, u32[]{:S(2)}) collective-permute-start(bf16[1280,512]{1,0:T(8,128)(2,1)S(1)} %get-tuple-element.1198), channel_id=1, source_target_pairs={{8,0},{16,8},{24,16},{9,1},{17,9},{25,17},{10,2},{18,10},{26,18},{... | collective-permute-start | bytes 3932168 | tf_op jit(solution)/shard_map/while/body/eval_jaxpr/ppermute | solution.py:12
  684.2 20.2 %collective-permute-start.1 = (bf16[1280,512]{1,0:T(8,128)(2,1)S(1)}, bf16[1280,512]{1,0:T(8,128)(2,1)}, u32[]{:S(2)}, u32[]{:S(2)}) collective-permute-start(bf16[1280,512]{1,0:T(8,128)(2,1)S(1)} %get-tuple-element.1198), channel_id=1, source_target_pairs={{8,0},{16,8},{24,16},{9,1},{17,9},{25,17},{10,2},{18,10},{26,18},{... | collective-permute-start | bytes 3932168 | tf_op jit(solution)/shard_map/while/body/eval_jaxpr/ppermute | solution.py:12
  724.8 20.5 %collective-permute-start.1 = (bf16[1280,512]{1,0:T(8,128)(2,1)S(1)}, bf16[1280,512]{1,0:T(8,128)(2,1)}, u32[]{:S(2)}, u32[]{:S(2)}) collective-permute-start(bf16[1280,512]{1,0:T(8,128)(2,1)S(1)} %get-tuple-element.1198), channel_id=1, source_target_pairs={{8,0},{16,8},{24,16},{9,1},{17,9},{25,17},{10,2},{18,10},{26,18},{... | collective-permute-start | bytes 3932168 | tf_op jit(solution)/shard_map/while/body/eval_jaxpr/ppermute | solution.py:12
  765.7 20.5 %collective-permute-start.1 = (bf16[1280,512]{1,0:T(8,128)(2,1)S(1)}, bf16[1280,512]{1,0:T(8,128)(2,1)}, u32[]{:S(2)}, u32[]{:S(2)}) collective-permute-start(bf16[1280,512]{1,0:T(8,128)(2,1)S(1)} %get-tuple-element.1198), channel_id=1, source_target_pairs={{8,0},{16,8},{24,16},{9,1},{17,9},{25,17},{10,2},{18,10},{26,18},{... | collective-permute-start | bytes 3932168 | tf_op jit(solution)/shard_map/while/body/eval_jaxpr/ppermute | solution.py:12
  786.2 193.9 %copy-start.2 = (bf16[1,771,512]{2,1,0:T(8,128)(2,1)S(1)}, bf16[1,771,512]{2,1,0:T(8,128)(2,1)}, u32[]{:S(2)}) copy-start(bf16[1,771,512]{2,1,0:T(8,128)(2,1)} %param.20) | copy-start | bytes 2368516
  786.8 193.2 %all-reduce.8.cloned.1.call-start = ((), (), s32[]{:S(2)}) async-start(), calls=%async_computation.1 | async-start | bytes 5275648 | tf_op jit(solution)/shard_map/psum | solution.py:216
  786.9 194.9 %copy-start.20 = (f32[512]{0:T(512)S(1)}, f32[512]{0:T(512)}, u32[]{:S(2)}) copy-start(f32[512]{0:T(512)} %copy-done.19) | copy-start | bytes 6148
  786.9 194.9 %copy-start.16 = (f32[1,512]{1,0:T(1,128)S(1)}, f32[1,512]{1,0:T(1,128)}, u32[]{:S(2)}) copy-start(f32[1,512]{1,0:T(1,128)} %copy-done.15) | copy-start | bytes 6148
  (101 other events, 455.0 us)
Sparse Core Ops, SparseCore 0:
  787.0 119.6 all-reduce.5
  909.7 70.3 all-reduce.7
where the time goes:
time: 999 us; the launch traced here: 994 us
  waiting for transfers between devices  524 us (52%)
  matrix products  248 us (25%)
  other arithmetic  75.6 us (8%)
  local copies, waits for them, and re-layouts  59.4 us (6%)
  starting transfers between devices  56.8 us (6%)
  between operations  14.4 us (1%)
  blocking collectives  14.2 us (1%)
    ppermute x18, waiting for transfers between devices, passed_along(): return lax.ppermute(block, axis, route)  346 us
    unnamed x3, waiting for transfers between devices  105 us
    dot_general x18, matrix products, layer_pair(): jnp.dot(active, weight_second, preferred_element_type=jnp.float32)  96.8 us
    psum x1, waiting for transfers between devices, shards(): lax.psum((grad_first, grad_second, bias_grad_first, bias_grad_second), 'dp')  72.1 us
    dot_general x27, matrix products, contract_rows(): lax.dot_general(left_side, right_side, (((0,), (0,)), ((), ())), preferre...  63.6 us
    dynamic_update_slice x18, other arithmetic, write_rows(): return lax.dynamic_update_slice_in_dim(target, chosen, first_row, 0)  63.2 us
    ppermute x18, starting transfers between devices, passed_along(): return lax.ppermute(block, axis, route)  56.7 us
    dot_general x18, matrix products, contract_cols(): lax.dot_general(left_side, right_side, (((1,), (1,)), ((), ())), preferre...  55.6 us
  transfers between devices with their start and end apart: 20, of which 20 were waited for; matrix products, arithmetic and copies ran while one was open for 7% of the time, Pallas kernels for 0%

commit v1 on v0

v1 whole, which is shorter than its diff:
```python
import functools

import jax
import jax.numpy as jnp
from jax import lax
from jax.experimental import pallas as pl
from jax.experimental.pallas import tpu as pltpu
from jax.sharding import PartitionSpec as P

BF = jnp.bfloat16
F32 = jnp.float32
NT = (((1,), (1,)), ((), ()))
TN = (((0,), (0,)), ((), ()))
SECTIONS = 4
ROWS = 960
SUB = 480
VMEM = 60 * 2**20


def up(value, step):
    return -(-value // step) * step


def mm(left, right, dims=(((1,), (0,)), ((), ()))):
    return lax.dot_general(left, right, dims, preferred_element_type=F32)


def silu_parts(half):
    half = half.astype(BF)
    lift = BF(1.0) + jnp.tanh(half)
    out = half * lift
    return out, lift + out * (BF(2.0) - lift)


def chain_kernel(
    width, extra, sc, h_in, g_in, ext, w_own, w_mine, w_other, b2,
    act, ig, h_keep, a_keep, og_keep, in_keep,
    hs, gs, mids, slope1, slope2, weights, sems,
):
    section, half = sc[0], sc[1]
    rows = h_in.shape[0]
    packed = weights.shape[1]
    part = packed // 2
    subs = [pl.ds(i, SUB) for i in range(0, rows, SUB)]
    first = pl.program_id(0) == 0

    def copies(k):
        slot = jnp.bitwise_xor(k, section)
        own = pltpu.make_async_copy(w_own, weights.at[k], sems.at[0, k])
        got = jnp.maximum(slot - 1, 0)
        mine = pltpu.make_async_copy(
            w_mine.at[got], weights.at[k, pl.ds(half * part, part)], sems.at[0, k]
        )
        other = pltpu.make_async_copy(
            w_other.at[got], weights.at[k, pl.ds((1 - half) * part, part)], sems.at[1, k]
        )
        return slot, own, mine, other

    def each(k, act_on):
        slot, own, mine, other = copies(k)

        @pl.when(slot == 0)
        def _():
            act_on(own)

        @pl.when(slot != 0)
        def _():
            act_on(mine)
            act_on(other)

    @pl.when(first)
    def _():
        for k in range(SECTIONS):
            each(k, lambda c: c.start())

    hs[0] = h_in[...]
    gs[SECTIONS] = g_in[...] * BF(0.5)

    def forward(k, unused):
        @pl.when(first)
        def _():
            each(k, lambda c: c.wait())

        for r in subs:
            z = mm(hs[k, r, :], weights[k, :width, :]) + mm(ext[r, :], weights[k, 2 * width :, :])
            out, slope = silu_parts(z)
            mids[k, r, :] = out
            slope1[k, r, :] = slope
            z = mm(out, weights[k, width : 2 * width, :]) + b2[k]
            out, slope = silu_parts(z)
            hs[k + 1, r, :] = out
            slope2[k, r, :] = slope
        return 0

    lax.fori_loop(0, SECTIONS, forward, 0)
    act[...] = hs[section + 1]
    h_keep[...] = hs[section]
    a_keep[...] = mids[section]

    def backward(j, unused):
        k = SECTIONS - 1 - j
        for r in subs:
            og = gs[k + 1, r, :] * slope2[k, r, :]
            slope2[k, r, :] = og
            back = mm(og, weights[k, width : 2 * width, :], NT)
            ing = (back * slope1[k, r, :].astype(F32)).astype(BF)
            slope1[k, r, :] = ing
            gs[k, r, :] = mm(ing, weights[k, :width, :], NT).astype(BF)
        return 0

    lax.fori_loop(0, SECTIONS - section, backward, 0)
    ig[...] = gs[section] * BF(2.0)
    og_keep[...] = slope2[section]
    in_keep[...] = slope1[section]


def run_chain(scalars, h, g, ext, w_own, w_mine, w_other, b2):
    total, width = h.shape
    extra = ext.shape[1]
    packed = w_own.shape[0]
    rows = lambda cols: pl.BlockSpec((ROWS, cols), lambda i, sc: (i, 0))
    hbm = pl.BlockSpec(memory_space=pl.ANY)
    out = jax.ShapeDtypeStruct((total, width), BF)
    block = lambda n: pltpu.VMEM((n, ROWS, width), BF)
    return pl.pallas_call(
        functools.partial(chain_kernel, width, extra),
        grid_spec=pltpu.PrefetchScalarGridSpec(
            num_scalar_prefetch=1,
            grid=(total // ROWS,),
            in_specs=[rows(width), rows(width), rows(extra), hbm, hbm, hbm,
                      pl.BlockSpec(b2.shape, lambda i, sc: (0, 0, 0))],
            out_specs=[rows(width)] * 6,
            scratch_shapes=[
                block(SECTIONS + 1), block(SECTIONS + 1), block(SECTIONS), block(SECTIONS), block(SECTIONS),
                pltpu.VMEM((SECTIONS, packed, width), BF),
                pltpu.SemaphoreType.DMA((2, SECTIONS)),
            ],
        ),
        out_shape=[out] * 6,
        compiler_params=pltpu.CompilerParams(vmem_limit_bytes=VMEM),
        cost_estimate=pl.CostEstimate(
            flops=2 * total * width * width * 20, bytes_accessed=total * width * 18,
            transcendentals=total * width * 8,
        ),
    )(scalars, h, g, ext, w_own, w_mine, w_other, b2)


def weight_kernel(width, cells, steps, h, a, og, ing, ext, out, acc1, acc2, acce, accb):
    step = pl.program_id(0)

    @pl.when(step == 0)
    def _():
        for acc in (acc1, acc2, acce, accb):
            acc[...] = jnp.zeros_like(acc)

    acc2[...] += mm(a[...], og[...], TN)
    acc1[...] += mm(h[...], ing[...], TN)
    acce[...] += mm(ext[...], ing[...], TN)
    accb[...] += jnp.sum(og[...].astype(F32).reshape(-1, 8, width), axis=0)

    @pl.when(step == steps - 1)
    def _():
        out[:width, :] = acc2[...].astype(BF)
        out[width : 2 * width, :] = acc1[...].astype(BF)
        last = jnp.sum(accb[...], axis=0, keepdims=True)
        row = lax.broadcasted_iota(jnp.int32, acce.shape, 0)
        out[2 * width :, :] = jnp.where(row == cells - 1, last, acce[...]).astype(BF)


def run_weight(h, a, og, ing, ext, cells):
    total, width = h.shape
    rows = lambda cols: pl.BlockSpec((ROWS, cols), lambda i: (i, 0))
    steps = total // ROWS
    packed = 2 * width + cells
    return pl.pallas_call(
        functools.partial(weight_kernel, width, cells, steps),
        grid=(steps,),
        in_specs=[rows(width)] * 4 + [rows(cells)],
        out_specs=pl.BlockSpec((packed, width), lambda i: (0, 0)),
        scratch_shapes=[pltpu.VMEM((width, width), F32), pltpu.VMEM((width, width), F32),
                        pltpu.VMEM((cells, width), F32), pltpu.VMEM((8, width), F32)],
        out_shape=jax.ShapeDtypeStruct((packed, width), BF),
        compiler_params=pltpu.CompilerParams(vmem_limit_bytes=VMEM),
        cost_estimate=pl.CostEstimate(
            flops=2 * total * packed * width, bytes_accessed=total * width * 9, transcendentals=0,
        ),
    )(h, a, og, ing, ext)


def swap_section(block, distance):
    route = [(i, i ^ distance) for i in range(lax.axis_size("section"))]
    return lax.ppermute(block, "section", route)


def swap_dp(block, distance):
    route = [(i, i ^ distance) for i in range(lax.axis_size("dp"))]
    return lax.ppermute(block, "dp", route)


def cut(array, first, count):
    return lax.dynamic_slice_in_dim(array, first, count, 0)


def sum_over_dp(packed):
    devices = lax.axis_size("dp")
    me = lax.axis_index("dp")
    core, place = me % 2, me // 2
    spots = devices // 2
    half = packed.shape[0] // 2
    piece = half // spots
    mine = cut(packed, core * half, half).astype(F32)
    theirs = swap_dp(cut(packed, (1 - core) * half, half), 1).astype(F32)
    chip = (mine + theirs).astype(BF)
    total = cut(chip, place * piece, piece).astype(F32)
    for distance in range(1, spots):
        away = jnp.bitwise_xor(place, distance)
        total = total + swap_dp(cut(chip, away * piece, piece), 2 * distance).astype(F32)
    total = total.astype(BF)
    slots = [total] + [swap_dp(total, 2 * distance) for distance in range(1, spots)]
    stack = jnp.stack(slots)
    other = swap_dp(stack, 1)
    order = jnp.bitwise_xor(jnp.arange(spots), place)
    both = jnp.stack([stack[order], other[order]]).reshape(2, half, -1)
    return jnp.where(core == 0, both, both[::-1]).reshape(packed.shape)


def norm_scale(direction, gain_row):
    norm = jnp.sqrt(jnp.sum(direction * direction, axis=0) + 1e-06)
    return norm


def weight_pullback(direction, gain_row, summed):
    norm = jnp.sqrt(jnp.sum(direction * direction, axis=0) + 1e-06)
    along = jnp.sum(direction * summed, axis=0)
    gain_grad = along / norm
    scale = gain_row / norm
    return scale[None, :] * summed - (scale * along / (norm * norm))[None, :] * direction, gain_grad


def shards(
    inputs, cotangent, latent_codes, positions, shape_ids,
    direction_first, gain_first, bias_first, direction_second, gain_second, bias_second,
):
    section = lax.axis_index("section")
    dp_rank = lax.axis_index("dp")
    dp_count = lax.axis_size("dp")
    core = dp_rank % 2
    total, width = inputs.shape
    shapes, latent = latent_codes.shape
    coords = positions.shape[0]
    cells = up(shapes + coords + 1, 128)
    dir_first = direction_first[0].astype(F32)
    dir_second = direction_second[0].astype(F32)
    gains_first = gain_first[0].astype(F32)
    gains_second = gain_second[0].astype(F32)

    def weight(direction, gain_row):
        scale = gain_row / jnp.sqrt(jnp.sum(direction * direction, axis=0) + 1e-06)
        return (direction * scale[None, :]).astype(BF)

    w1 = weight(dir_first, gains_first)
    w2 = weight(dir_second, gains_second)
    w_skip = w1[width : width + latent]
    by_shape = 0.5 * (mm(latent_codes, w_skip) + bias_first[0].astype(F32)[None, :])
    by_shape_high = by_shape.astype(BF)
    by_shape_low = (by_shape - by_shape_high.astype(F32)).astype(BF)
    half = BF(0.5)
    pad = lambda count: jnp.zeros((count, width), BF)
    packed = jnp.concatenate([
        w1[:width] * half, w2 * half,
        by_shape_high, w1[width + latent :] * half, pad(cells - shapes - coords - 1), bias_second * half,
        by_shape_low, pad(cells - shapes),
    ])
    part = packed.shape[0] // 2
    sending = cut(packed, core * part, part)
    mine = jnp.stack([swap_section(sending, d) for d in range(1, SECTIONS)])
    other = swap_dp(mine, 1)
    spot = 2 * width + cells - 1
    in_part = spot - part
    others_b2 = jnp.where(core == 1, mine[:, in_part], other[:, in_part])
    b2_slots = jnp.concatenate([bias_second * half, others_b2]).astype(F32)
    b2 = b2_slots[jnp.bitwise_xor(jnp.arange(SECTIONS), section)][:, None, :]

    onehot = (shape_ids[:, None] == jnp.arange(shapes, dtype=jnp.int32)[None, :]).astype(BF)
    blank = lambda count: jnp.zeros((total, count), BF)
    ext = jnp.concatenate(
        [onehot, positions.T, blank(cells - shapes - coords), onehot, blank(cells - shapes)], axis=1
    )

    scalars = jnp.stack([section, core]).astype(jnp.int32)
    act, ig, h_keep, a_keep, og_keep, in_keep = run_chain(
        scalars, inputs, cotangent, ext, packed, mine, other, b2
    )
    partial = run_weight(h_keep, a_keep, og_keep, in_keep, ext, cells)
    summed = sum_over_dp(partial).astype(F32)
    sum_second = summed[:width]
    grid = summed[2 * width : 2 * width + shapes]
    places = summed[2 * width + shapes : 2 * width + shapes + coords]
    bias_sum_second = summed[2 * width + cells - 1]
    bias_sum_first = jnp.sum(grid, axis=0)
    grid_low = grid.astype(BF)
    skip_sum = mm(latent_codes, grid_low, TN)
    sum_first = jnp.concatenate([summed[width : 2 * width], skip_sum, places])
    dir_grad_first, gain_grad_first = weight_pullback(dir_first, gains_first, sum_first)
    dir_grad_second, gain_grad_second = weight_pullback(dir_second, gains_second, sum_second)
    code_part = mm(grid_low, w_skip, NT)
    owned = shapes // (SECTIONS * dp_count)
    code = cut(code_part, (section * dp_count + dp_rank) * owned, owned)
    for distance in range(1, SECTIONS):
        away = jnp.bitwise_xor(section, distance)
        code = code + swap_section(cut(code_part, (away * dp_count + dp_rank) * owned, owned), distance)
    return (
        act[None], ig[None], code,
        dir_grad_first[None], gain_grad_first[None], bias_sum_first[None],
        dir_grad_second[None], gain_grad_second[None], bias_sum_second[None],
    )


def solution(mesh):
    in_specs = (
        P("dp", None), P("dp", None), P(), P(None, "dp"), P("dp"),
        P("section", None, None), P("section", None), P("section", None),
        P("section", None, None), P("section", None), P("section", None),
    )
    out_specs = (
        P("section", "dp", None), P("section", "dp", None), P(("section", "dp"), None),
        P("section", None, None), P("section", None), P("section", None),
        P("section", None, None), P("section", None), P("section", None),
    )
    return jax.shard_map(shards, mesh=mesh, in_specs=in_specs, out_specs=out_specs, check_vma=False)
```

time: 999 us -> 242 us (0.24)
  waiting for transfers between devices: 524 us -> 52.4 us
  matrix products: 248 us -> 0.63 us
  Pallas kernels: 0 us -> 124 us
  other arithmetic: 75.6 us -> 19.1 us
  starting transfers between devices: 56.8 us -> 18.6 us
  local copies, waits for them, and re-layouts: 59.4 us -> 25.8 us
  blocking collectives: 14.2 us -> 0 us
  between operations: 14.4 us -> 1.03 us
    ppermute x18 -> x15, waiting for transfers between devices: 346 us -> 52.4 us  [the longest x6 27 us: swap_section(): return lax.ppermute(block, 'section', route)]
    dot_general x90 -> x3, matrix products: 248 us -> 0.63 us  [mm(): return lax.dot_general(left, right, dims, preferred_element_type=F32)]
    pallas_call x0 -> x2, Pallas kernels: none -> 124 us  [the longest x1 106 us: run_chain(): pl.pallas_call(functools.partial(chain_kernel, width, extra), grid_spec=p...]
    unnamed x3 -> x0, waiting for transfers between devices: 105 us -> none
    psum x1 -> x0, waiting for transfers between devices: 72.1 us -> none  [shards(): lax.psum((grad_first, grad_second, bias_grad_first, bias_grad_second), 'dp')]
    dynamic_update_slice x18 -> x0, other arithmetic: 63.2 us -> none  [write_rows(): return lax.dynamic_update_slice_in_dim(target, chosen, first_row, 0)]
    ppermute x18 -> x15, starting transfers between devices: 56.7 us -> 18.6 us  [the longest x9 10.5 us: swap_dp(): return lax.ppermute(block, 'dp', route)]
    transpose x18 -> x0, local copies, waits for them, and re-layouts: 24.4 us -> none  [layer_pair(): joined = jnp.concatenate([entering, skip_rows, place_rows.T], axis=1)]
  transfers between devices with their start and end apart: 20 -> 15, of which waited for: 20 -> 8; matrix products, arithmetic and copies ran while one was open for 7% -> 11% of each run, Pallas kernels for 0% -> 0%
where the time goes in v1:
time: 242 us; the launch traced here: 241 us
  Pallas kernels  124 us (51%)
  waiting for transfers between devices  52.4 us (22%)
  local copies, waits for them, and re-layouts  25.8 us (11%)
  other arithmetic  19.1 us (8%)
  starting transfers between devices  18.6 us (8%)
    pallas_call x1, Pallas kernels, run_chain(): pl.pallas_call(functools.partial(chain_kernel, width, extra), grid_spec=p...  106 us
    ppermute x6, waiting for transfers between devices, swap_section(): return lax.ppermute(block, 'section', route)  27 us
    ppermute x9, waiting for transfers between devices, swap_dp(): return lax.ppermute(block, 'dp', route)  25.4 us
    pallas_call x1, Pallas kernels, run_weight(): pl.pallas_call(functools.partial(weight_kernel, width, cells, steps), gri...  17.4 us
    concatenate x1, local copies, waits for them, and re-layouts, shards(): jnp.concatenate([onehot, positions.T, blank(cells - shapes - coords), one...  11.6 us
    ppermute x9, starting transfers between devices, swap_dp(): return lax.ppermute(block, 'dp', route)  10.5 us
    ppermute x6, starting transfers between devices, swap_section(): return lax.ppermute(block, 'section', route)  8.08 us
  transfers between devices with their start and end apart: 15, of which 8 were waited for; matrix products, arithmetic and copies ran while one was open for 11% of the time, Pallas kernels for 0%

profile of v1, /device:TPU:0, one launch (start us, length us, event | category | flops | bytes accessed | tf_op | source)
XLA Modules:
  0.0 241.3 jit_solution(8372519636325855140)
XLA Ops:
  0.7 1.4 fusion.4
  5.6 2.3 concatenate.29.w_own
  8.0 3.0 %collective-permute-start = (bf16[640,512]{1,0:T(8,128)(2,1)S(1)}, bf16[640,512]{1,0:T(8,128)(2,1)}, u32[]{:S(2)}, u32[]{:S(2)}) collective-permute-start(bf16[640,512]{1,0:T(8,128)(2,1)S(1)} %constant_dynamic-slice_fusion.8), channel_id=1, source_target_pairs={{0,8},{8,0},{16,24},{24,16},{1,9},{9,1},{17,25},{25,17},{2,10},{10... | collective-permute-start | bytes 1966088 | tf_op jit(solution)/shard_map/ppermute | solution.py:192
  11.0 1.5 collective-permute-start.1
  12.5 1.8 copy.22
  14.3 12.4 %collective-permute-done = bf16[640,512]{1,0:T(8,128)(2,1)} collective-permute-done((bf16[640,512]{1,0:T(8,128)(2,1)S(1)}, bf16[640,512]{1,0:T(8,128)(2,1)}, u32[]{:S(2)}, u32[]{:S(2)}) %collective-permute-start) | collective-permute-done | bytes 655392 | tf_op jit(solution)/shard_map/ppermute | solution.py:192
  26.7 14.7 %collective-permute-done.1 = bf16[640,512]{1,0:T(8,128)(2,1)} collective-permute-done((bf16[640,512]{1,0:T(8,128)(2,1)S(1)}, bf16[640,512]{1,0:T(8,128)(2,1)}, u32[]{:S(2)}, u32[]{:S(2)}) %collective-permute-start.1) | collective-permute-done | bytes 655392 | tf_op jit(solution)/shard_map/ppermute | solution.py:192
  41.3 3.0 %pad_maximum_fusion.w_mine = bf16[3,640,512]{2,1,0:T(8,128)(2,1)} fusion(bf16[1,640,512]{2,1,0:T(8,128)(2,1)} %bitcast.14, bf16[1,640,512]{2,1,0:T(8,128)(2,1)} %bitcast.13, bf16[1,640,512]{2,1,0:T(8,128)(2,1)} %bitcast.12), kind=kLoop, calls=%fused_computation.10 | loop fusion | flops 1966080 | bytes 3932160 | tf_op jit(solution)/shard_map/stack | solution.py:276
  44.4 3.5 %fusion = bf16[7680,64]{1,0:T(8,128)(2,1)S(1)} fusion(s32[7680]{0:T(1024)S(1)} %copy-done.6), kind=kLoop, calls=%fused_computation.4 | loop fusion | flops 983040 | bytes 1013760 | tf_op jit(solution)/shard_map/convert_element_type | solution.py:284
  47.9 1.5 broadcast_in_dim.18
  49.4 1.5 broadcast_in_dim.19
  50.9 11.6 %concatenate.28.ext = bf16[7680,256]{1,0:T(8,128)(2,1)} concatenate(bf16[7680,64]{1,0:T(8,128)(2,1)S(1)} %fusion, bf16[7680,3]{1,0:T(8,128)(2,1)} %bitcast.69, bf16[7680,61]{1,0:T(8,128)(2,1)} %broadcast_in_dim.18, bf16[7680,64]{1,0:T(8,128)(2,1)S(1)} %fusion, bf16[7680,64]{1,0:T(8,128)(2,1)} %broadcast_in_dim.19), dimensions={1} | concatenate | bytes 7864320 | tf_op jit(solution)/shard_map/concatenate | solution.py:286
  65.1 106.4 %shard_map.178 = (bf16[7680,512]{1,0:T(8,128)(2,1)}, bf16[7680,512]{1,0:T(8,128)(2,1)}, bf16[7680,512]{1,0:T(8,128)(2,1)}, bf16[7680,512]{1,0:T(8,128)(2,1)}, bf...) custom-call(s32[2]{0:T(128)} %pad_add_fusion.sc, bf16[7680,512]{1,0:T(8,128)(2,1)} %h_in.1, bf16[7680,512]{1,0:T(8,128)(2,1)} %g_in.1, ...), custom_call_target="tpu_custom_call" | custom-call | flops 80530636800 | bytes 70778880 | tf_op jit(solution)/shard_map/pallas_call | solution.py:125
  171.5 17.4 %shard_map.179 = bf16[1152,512]{1,0:T(8,128)(2,1)} custom-call(bf16[7680,512]{1,0:T(8,128)(2,1)} %get-tuple-element.17.h, bf16[7680,512]{1,0:T(8,128)(2,1)} %get-tuple-element.18.a, bf16[7680,512]{1,0:T(8,128)(2,1)} %get-tuple-element.19.og, bf16[7680,512]{1,0:T(8,128)(2,1)} %get-tuple-element.20.ing, bf16[7680,256]{1,0:T(8,128)(2,1)} %concatenate.28.ext), custom_call_target="tpu_custom_call" | custom-call | flops 9059696640 | bytes 35389440 | tf_op jit(solution)/shard_map/pallas_call | solution.py:175
  190.6 1.8 collective-permute-done.4
  193.7 1.7 collective-permute-start.5
  195.3 2.6 %collective-permute-start.6 = (bf16[144,512]{1,0:T(8,128)(2,1)S(1)}, bf16[144,512]{1,0:T(8,128)(2,1)S(1)}, u32[]{:S(2)}, u32[]{:S(2)}) collective-permute-start(bf16[144,512]{1,0:T(8,128)(2,1)S(1)} %get-tuple-element.48), channel_id=1, source_target_pairs={{0,4},{1,5},{2,6},{3,7},{4,0},{5,1},{6,2},{7,3},{8,12},{9,13},{10,... | collective-permute-start | bytes 442376 | tf_op jit(solution)/shard_map/ppermute | solution.py:197
  198.1 4.4 %collective-permute-done.5 = bf16[144,512]{1,0:T(8,128)(2,1)S(1)} collective-permute-done((bf16[144,512]{1,0:T(8,128)(2,1)S(1)}, bf16[144,512]{1,0:T(8,128)(2,1)S(1)}, u32[]{:S(2)}, u32[]{:S(2)}) %collective-permute-start.5) | collective-permute-done | bytes 147488 | tf_op jit(solution)/shard_map/ppermute | solution.py:197
  202.5 6.8 %collective-permute-done.6 = bf16[144,512]{1,0:T(8,128)(2,1)S(1)} collective-permute-done((bf16[144,512]{1,0:T(8,128)(2,1)S(1)}, bf16[144,512]{1,0:T(8,128)(2,1)S(1)}, u32[]{:S(2)}, u32[]{:S(2)}) %collective-permute-start.6) | collective-permute-done | bytes 147488 | tf_op jit(solution)/shard_map/ppermute | solution.py:197
  209.4 2.9 %collective-permute-start.8 = (bf16[144,512]{1,0:T(8,128)(2,1)S(1)}, bf16[144,512]{1,0:T(8,128)(2,1)S(1)}, u32[]{:S(2)}, u32[]{:S(2)}) collective-permute-start(bf16[144,512]{1,0:T(8,128)(2,1)S(1)} %add_convert_fusion.1), channel_id=1, source_target_pairs={{0,2},{1,3},{2,0},{3,1},{4,6},{5,7},{6,4},{7,5},{8,10},{9,11},{10,... | collective-permute-start | bytes 442376 | tf_op jit(solution)/shard_map/ppermute | solution.py:197
  214.8 2.4 %collective-permute-done.8 = bf16[144,512]{1,0:T(8,128)(2,1)S(1)} collective-permute-done((bf16[144,512]{1,0:T(8,128)(2,1)S(1)}, bf16[144,512]{1,0:T(8,128)(2,1)S(1)}, u32[]{:S(2)}, u32[]{:S(2)}) %collective-permute-start.8) | collective-permute-done | bytes 147488 | tf_op jit(solution)/shard_map/ppermute | solution.py:197
  217.2 8.7 %collective-permute-done.9 = bf16[144,512]{1,0:T(8,128)(2,1)S(1)} collective-permute-done((bf16[144,512]{1,0:T(8,128)(2,1)S(1)}, bf16[144,512]{1,0:T(8,128)(2,1)S(1)}, u32[]{:S(2)}, u32[]{:S(2)}) %collective-permute-start.9) | collective-permute-done | bytes 147488 | tf_op jit(solution)/shard_map/ppermute | solution.py:197
  232.2 3.4 %collective-permute-start.14 = (f32[2,256]{1,0:T(2,128)S(1)}, f32[2,256]{1,0:T(2,128)S(1)}, u32[]{:S(2)}, u32[]{:S(2)}) collective-permute-start(f32[2,256]{1,0:T(2,128)S(1)} %get-tuple-element.50), channel_id=1, source_target_pairs={{0,24},{8,16},{16,8},{24,0},{1,25},{9,17},{17,9},{25,1},{2,26},{10... | collective-permute-start | bytes 6152 | tf_op jit(solution)/shard_map/ppermute | solution.py:192
  237.9 2.8 %copy.23 = f32[1,771,512]{2,0,1:T(1,128)} copy(f32[1,771,512]{2,1,0:T(8,128)S(1)} %fusion.7) | data formatting | bytes 3158016
  (84 shorter events, 21.0 us)
Async XLA Ops:
  0.6 4.7 %copy-start = (bf16[64,256]{1,0:T(8,128)(2,1)S(1)}, bf16[64,256]{1,0:T(8,128)(2,1)}, u32[]{:S(2)}) copy-start(bf16[64,256]{1,0:T(8,128)(2,1)} %param.13) | copy-start | bytes 98308
  0.7 3.4 %copy-start.2 = (bf16[1,512,512]{2,1,0:T(8,128)(2,1)S(1)}, bf16[1,512,512]{2,1,0:T(8,128)(2,1)}, u32[]{:S(2)}) copy-start(bf16[1,512,512]{2,1,0:T(8,128)(2,1)} %param.19) | copy-start | bytes 1572868
  0.7 3.6 %copy-start.7 = (bf16[1,512]{1,0:T(2,128)(2,1)S(1)}, bf16[1,512]{1,0:T(2,128)(2,1)}, u32[]{:S(2)}) copy-start(bf16[1,512]{1,0:T(2,128)(2,1)} %param.20) | copy-start | bytes 3076
  4.1 1.3 copy-start.8
  5.6 7.0 %copy-start.5 = (bf16[3,7680]{1,0:T(4,128)(2,1)S(1)}, bf16[3,7680]{1,0:T(4,128)(2,1)}, u32[]{:S(2)}) copy-start(bf16[3,7680]{1,0:T(4,128)(2,1)} %param.14) | copy-start | bytes 138244
  7.9 6.4 %copy-start.4 = (bf16[1280,512]{1,0:T(8,128)(2,1)}, bf16[1280,512]{1,0:T(8,128)(2,1)S(1)}, u32[]{:S(2)}) copy-start(bf16[1280,512]{1,0:T(8,128)(2,1)S(1)} %concatenate.29.w_own) | copy-start | bytes 3932164
  8.0 18.7 %collective-permute-start = (bf16[640,512]{1,0:T(8,128)(2,1)S(1)}, bf16[640,512]{1,0:T(8,128)(2,1)}, u32[]{:S(2)}, u32[]{:S(2)}) collective-permute-start(bf16[640,512]{1,0:T(8,128)(2,1)S(1)} %constant_dynamic-slice_fusion.8), channel_id=1, source_target_pairs={{0,8},{8,0},{16,24},{24,16},{1,9},{9,1},{17,25},{25,17},{2,10},{10... | collective-permute-start | bytes 1966088 | tf_op jit(solution)/shard_map/ppermute | solution.py:192
  11.0 30.3 %collective-permute-start.1 = (bf16[640,512]{1,0:T(8,128)(2,1)S(1)}, bf16[640,512]{1,0:T(8,128)(2,1)}, u32[]{:S(2)}, u32[]{:S(2)}) collective-permute-start(bf16[640,512]{1,0:T(8,128)(2,1)S(1)} %constant_dynamic-slice_fusion.8), channel_id=1, source_target_pairs={{0,16},{8,24},{16,0},{24,8},{1,17},{9,25},{17,1},{25,9},{2,18},{10... | collective-permute-start | bytes 1966088 | tf_op jit(solution)/shard_map/ppermute | solution.py:192
  12.5 28.8 %collective-permute-start.2 = (bf16[640,512]{1,0:T(8,128)(2,1)S(1)}, bf16[640,512]{1,0:T(8,128)(2,1)}, u32[]{:S(2)}, u32[]{:S(2)}) collective-permute-start(bf16[640,512]{1,0:T(8,128)(2,1)S(1)} %constant_dynamic-slice_fusion.8), channel_id=1, source_target_pairs={{0,24},{8,16},{16,8},{24,0},{1,25},{9,17},{17,9},{25,1},{2,26},{10... | collective-permute-start | bytes 1966088 | tf_op jit(solution)/shard_map/ppermute | solution.py:192
  41.3 3.0 %copy-start.6 = (s32[7680]{0:T(1024)S(1)}, s32[7680]{0:T(1024)}, u32[]{:S(2)}) copy-start(s32[7680]{0:T(1024)} %param.15) | copy-start | bytes 92164
  44.4 18.7 %collective-permute-start.3 = (bf16[3,640,512]{2,1,0:T(8,128)(2,1)}, bf16[3,640,512]{2,1,0:T(8,128)(2,1)}, u32[]{:S(2)}, u32[]{:S(2)}) collective-permute-start(bf16[3,640,512]{2,1,0:T(8,128)(2,1)} %pad_maximum_fusion.w_mine), channel_id=1, source_target_pairs={{0,1},{1,0},{2,3},{3,2},{4,5},{5,4},{6,7},{7,6},{8,9},{9,8},{10,11... | collective-permute-start | bytes 5898248 | tf_op jit(solution)/shard_map/ppermute | solution.py:197
  188.9 3.5 %copy-start.3 = (bf16[1152,512]{1,0:T(8,128)(2,1)S(1)}, bf16[1152,512]{1,0:T(8,128)(2,1)}, u32[]{:S(2)}) copy-start(bf16[1152,512]{1,0:T(8,128)(2,1)} %shard_map.179) | copy-start | bytes 3538948
  190.1 2.3 collective-permute-start.4
  193.7 8.8 %collective-permute-start.5 = (bf16[144,512]{1,0:T(8,128)(2,1)S(1)}, bf16[144,512]{1,0:T(8,128)(2,1)S(1)}, u32[]{:S(2)}, u32[]{:S(2)}) collective-permute-start(bf16[144,512]{1,0:T(8,128)(2,1)S(1)} %get-tuple-element.46), channel_id=1, source_target_pairs={{0,2},{1,3},{2,0},{3,1},{4,6},{5,7},{6,4},{7,5},{8,10},{9,11},{10,... | collective-permute-start | bytes 442376 | tf_op jit(solution)/shard_map/ppermute | solution.py:197
  195.3 14.0 %collective-permute-start.6 = (bf16[144,512]{1,0:T(8,128)(2,1)S(1)}, bf16[144,512]{1,0:T(8,128)(2,1)S(1)}, u32[]{:S(2)}, u32[]{:S(2)}) collective-permute-start(bf16[144,512]{1,0:T(8,128)(2,1)S(1)} %get-tuple-element.48), channel_id=1, source_target_pairs={{0,4},{1,5},{2,6},{3,7},{4,0},{5,1},{6,2},{7,3},{8,12},{9,13},{10,... | collective-permute-start | bytes 442376 | tf_op jit(solution)/shard_map/ppermute | solution.py:197
  197.9 11.4 %collective-permute-start.7 = (bf16[144,512]{1,0:T(8,128)(2,1)S(1)}, bf16[144,512]{1,0:T(8,128)(2,1)S(1)}, u32[]{:S(2)}, u32[]{:S(2)}) collective-permute-start(bf16[144,512]{1,0:T(8,128)(2,1)S(1)} %get-tuple-element.47), channel_id=1, source_target_pairs={{0,6},{1,7},{2,4},{3,5},{4,2},{5,3},{6,0},{7,1},{8,14},{9,15},{10,... | collective-permute-start | bytes 442376 | tf_op jit(solution)/shard_map/ppermute | solution.py:197
  209.4 7.8 %collective-permute-start.8 = (bf16[144,512]{1,0:T(8,128)(2,1)S(1)}, bf16[144,512]{1,0:T(8,128)(2,1)S(1)}, u32[]{:S(2)}, u32[]{:S(2)}) collective-permute-start(bf16[144,512]{1,0:T(8,128)(2,1)S(1)} %add_convert_fusion.1), channel_id=1, source_target_pairs={{0,2},{1,3},{2,0},{3,1},{4,6},{5,7},{6,4},{7,5},{8,10},{9,11},{10,... | collective-permute-start | bytes 442376 | tf_op jit(solution)/shard_map/ppermute | solution.py:197
  212.3 13.6 %collective-permute-start.9 = (bf16[144,512]{1,0:T(8,128)(2,1)S(1)}, bf16[144,512]{1,0:T(8,128)(2,1)S(1)}, u32[]{:S(2)}, u32[]{:S(2)}) collective-permute-start(bf16[144,512]{1,0:T(8,128)(2,1)S(1)} %add_convert_fusion.1), channel_id=1, source_target_pairs={{0,4},{1,5},{2,6},{3,7},{4,0},{5,1},{6,2},{7,3},{8,12},{9,13},{10,... | collective-permute-start | bytes 442376 | tf_op jit(solution)/shard_map/ppermute | solution.py:197
  213.4 12.5 %collective-permute-start.10 = (bf16[144,512]{1,0:T(8,128)(2,1)S(1)}, bf16[144,512]{1,0:T(8,128)(2,1)S(1)}, u32[]{:S(2)}, u32[]{:S(2)}) collective-permute-start(bf16[144,512]{1,0:T(8,128)(2,1)S(1)} %add_convert_fusion.1), channel_id=1, source_target_pairs={{0,6},{1,7},{2,4},{3,5},{4,2},{5,3},{6,0},{7,1},{8,14},{9,15},{10,... | collective-permute-start | bytes 442376 | tf_op jit(solution)/shard_map/ppermute | solution.py:197
  225.9 2.1 collective-permute-start.11
  230.6 4.9 %copy-start.1 = (bf16[1,771,512]{2,1,0:T(8,128)(2,1)S(1)}, bf16[1,771,512]{2,1,0:T(8,128)(2,1)}, u32[]{:S(2)}) copy-start(bf16[1,771,512]{2,1,0:T(8,128)(2,1)} %param.16) | copy-start | bytes 2368516
  232.0 8.7 %collective-permute-start.12 = (f32[2,256]{1,0:T(2,128)S(1)}, f32[2,256]{1,0:T(2,128)S(1)}, u32[]{:S(2)}, u32[]{:S(2)}) collective-permute-start(f32[2,256]{1,0:T(2,128)S(1)} %get-tuple-element.49), channel_id=1, source_target_pairs={{0,8},{8,0},{16,24},{24,16},{1,9},{9,1},{17,25},{25,17},{2,10},{10... | collective-permute-start | bytes 6152 | tf_op jit(solution)/shard_map/ppermute | solution.py:192
  232.1 8.6 %collective-permute-start.13 = (f32[2,256]{1,0:T(2,128)S(1)}, f32[2,256]{1,0:T(2,128)S(1)}, u32[]{:S(2)}, u32[]{:S(2)}) collective-permute-start(f32[2,256]{1,0:T(2,128)S(1)} %get-tuple-element.51), channel_id=1, source_target_pairs={{0,16},{8,24},{16,0},{24,8},{1,17},{9,25},{17,1},{25,9},{2,18},{10... | collective-permute-start | bytes 6152 | tf_op jit(solution)/shard_map/ppermute | solution.py:192
  232.2 8.5 %collective-permute-start.14 = (f32[2,256]{1,0:T(2,128)S(1)}, f32[2,256]{1,0:T(2,128)S(1)}, u32[]{:S(2)}, u32[]{:S(2)}) collective-permute-start(f32[2,256]{1,0:T(2,128)S(1)} %get-tuple-element.50), channel_id=1, source_target_pairs={{0,24},{8,16},{16,8},{24,0},{1,25},{9,17},{17,9},{25,1},{2,26},{10... | collective-permute-start | bytes 6152 | tf_op jit(solution)/shard_map/ppermute | solution.py:192
  (1 other events, 1.2 us)
